TPU v7x, 512 devices: a whole 4x8x8 slice. The times are simulated.
512 devices in a mesh: dp: 512 (over x, y, z, core).
Axes of the slice: x: 4, y: 8, z: 8, core: 2. Of those that a mesh axis runs over, the one named last changes fastest.
Arguments:
- image_emb: bfloat16 [131072, 1152], P('dp'), may hold values from -0.1875 to 0.1875
- text_emb: bfloat16 [131072, 1152], P('dp'), may hold values from -0.1875 to 0.1875
- pair_id: int32 [131072], P('dp'), may hold values from 0 to 32767
- logit_scale: float32 [1], replicated, may hold values from 6 to 14
- logit_bias: float32 [1], replicated, may hold values from -4 to -1
Outputs:
- image_grad: float32 [131072, 1152], P('dp')
- text_grad: float32 [131072, 1152], P('dp')
All inputs are finite; a program needn't handle non-finite values.
Results may differ from a plain program's by a relative error of at most 0.0045.
Values may be sent and summed in bfloat16 or wider, within the bound.
A program may use at most 64 MiB of HBM per device.

v0:
```python
import jax
import jax.numpy as jnp
from jax import lax
from jax.sharding import PartitionSpec as P

ROUNDS = 3


def from_behind(value, axis, steps):
    count = lax.axis_size(axis)
    pairs = [(source, (source + steps) % count) for source in range(count)]
    return lax.ppermute(value, axis, pairs)


def normalize(embedding):
    as_float = embedding.astype(jnp.float32)
    row_norms = jnp.sqrt(jnp.sum(as_float * as_float, axis=1, keepdims=True) + 1e-06)
    return (as_float / row_norms, row_norms)


def block_coeff(left_rows, right_rows, left_ids, right_ids, scale_value, bias_value):
    scores = jnp.dot(left_rows, right_rows.T, preferred_element_type=jnp.float32)
    logits = scale_value * scores + bias_value
    positive = (left_ids[:, None] == right_ids[None, :]).astype(jnp.float32)
    return (scale_value * (jax.nn.sigmoid(logits) - positive)).astype(jnp.bfloat16)


def product(left_rows, right_rows):
    return jnp.dot(left_rows, right_rows, preferred_element_type=jnp.float32)


def per_device(image_emb, text_emb, pair_id, logit_scale, logit_bias):
    scale_value = logit_scale[0]
    bias_value = logit_bias[0]
    unit_img, norm_img = normalize(image_emb)
    unit_txt, norm_txt = normalize(text_emb)
    img_hat = unit_img.astype(jnp.bfloat16)
    txt_hat = unit_txt.astype(jnp.bfloat16)
    own_block = block_coeff(img_hat, txt_hat, pair_id, pair_id, scale_value, bias_value)
    grad_img = product(own_block, txt_hat)
    grad_txt = product(own_block.T, img_hat)
    devices = lax.axis_size("dp")
    for round_index in range(ROUNDS):
        distance = 1 + round_index * (devices // 6)
        far_img, far_txt, far_ids = from_behind((img_hat, txt_hat, pair_id), "dp", distance)
        near_block = block_coeff(img_hat, far_txt, pair_id, far_ids, scale_value, bias_value)
        grad_img = grad_img + product(near_block, far_txt)
        back_txt = product(near_block.T, img_hat)
        mirror_block = block_coeff(far_img, txt_hat, far_ids, pair_id, scale_value, bias_value)
        grad_txt = grad_txt + product(mirror_block.T, far_img)
        back_img = product(mirror_block, txt_hat)
        return_img, return_txt = (
            from_behind(back_img.astype(jnp.bfloat16), "dp", -distance).astype(back_img.dtype),
            from_behind(back_txt.astype(jnp.bfloat16), "dp", -distance).astype(back_txt.dtype),
        )
        grad_img = grad_img + return_img
        grad_txt = grad_txt + return_txt
    image_grad = (
        grad_img - unit_img * jnp.sum(unit_img * grad_img, axis=1, keepdims=True)
    ) / norm_img
    text_grad = (
        grad_txt - unit_txt * jnp.sum(unit_txt * grad_txt, axis=1, keepdims=True)
    ) / norm_txt
    return (image_grad, text_grad)


def solution(mesh):
    in_specs = (P("dp", None), P("dp", None), P("dp"), P(), P())
    out_specs = (P("dp", None), P("dp", None))
    return jax.shard_map(
        per_device, mesh=mesh, in_specs=in_specs, out_specs=out_specs, check_vma=False
    )
```

profile of v0, /device:TPU:131, one launch (start us, length us, event | category | flops | bytes accessed | tf_op | source)
XLA Modules:
  0.0 288.2 jit_solution(3047791433562510090)
XLA Ops:
  0.6 12.5 %collective-permute-start.5 = (s32[256]{0:T(256)}, s32[256]{0:T(256)S(1)}, u32[]{:S(2)}, u32[]{:S(2)}) collective-permute-start(s32[256]{0:T(256)} %param.7), channel_id=1, source_target_pairs={{0,86},{1,87},{2,88},{3,89},{4,90},{5,91},{6,92},{7,93},{8,94},{9,... | collective-permute-start | bytes 3080 | tf_op jit(solution)/shard_map/ppermute | solution.py:12
  13.2 3.9 %collective-permute-start.1 = (s32[256]{0:T(256)}, s32[256]{0:T(256)S(1)}, u32[]{:S(2)}, u32[]{:S(2)}) collective-permute-start(s32[256]{0:T(256)} %param.7), channel_id=1, source_target_pairs={{0,1},{1,2},{2,3},{3,4},{4,5},{5,6},{6,7},{7,8},{8,9},{9,10},{10,1... | collective-permute-start | bytes 3080 | tf_op jit(solution)/shard_map/ppermute | solution.py:12
  17.1 1.3 fusion.11
  18.4 1.3 fusion.69
  19.7 1.9 collective-permute-start
  21.6 1.9 collective-permute-start.4
  24.0 7.3 %collective-permute-start.6 = (bf16[256,1152]{1,0:T(8,128)(2,1)S(1)}, bf16[256,1152]{1,0:T(8,128)(2,1)S(1)}, u32[]{:S(2)}, u32[]{:S(2)}) collective-permute-start(bf16[256,1152]{1,0:T(8,128)(2,1)S(1)} %fusion.68), channel_id=1, source_target_pairs={{0,86},{1,87},{2,88},{3,89},{4,90},{5,91},{6,92},{7,93},{8,94},{9,... | collective-permute-start | bytes 1769480 | tf_op jit(solution)/shard_map/ppermute | solution.py:12
  33.8 4.7 %collective-permute-start.10 = (bf16[256,1152]{1,0:T(8,128)(2,1)S(1)}, bf16[256,1152]{1,0:T(8,128)(2,1)S(1)}, u32[]{:S(2)}, u32[]{:S(2)}) collective-permute-start(bf16[256,1152]{1,0:T(8,128)(2,1)S(1)} %fusion.68), channel_id=1, source_target_pairs={{0,171},{1,172},{2,173},{3,174},{4,175},{5,176},{6,177},{7,178},{8... | collective-permute-start | bytes 1769480 | tf_op jit(solution)/shard_map/ppermute | solution.py:12
  38.5 13.2 %collective-permute-done = bf16[256,1152]{1,0:T(8,128)(2,1)S(1)} collective-permute-done((bf16[256,1152]{1,0:T(8,128)(2,1)S(1)}, bf16[256,1152]{1,0:T(8,128)(2,1)S(1)}, u32[]{:S(2)}, u32[]{:S(2)}) %collective-permute-start) | collective-permute-done | bytes 589856 | tf_op jit(solution)/shard_map/ppermute | solution.py:12
  51.7 1.9 collective-permute-start.8
  53.6 0.4 fusion.62
  54.4 1.9 collective-permute-start.9
  56.3 11.1 %collective-permute-done.4 = bf16[256,1152]{1,0:T(8,128)(2,1)S(1)} collective-permute-done((bf16[256,1152]{1,0:T(8,128)(2,1)S(1)}, bf16[256,1152]{1,0:T(8,128)(2,1)S(1)}, u32[]{:S(2)}, u32[]{:S(2)}) %collective-permute-start.4) | collective-permute-done | bytes 589856 | tf_op jit(solution)/shard_map/ppermute | solution.py:12
  67.4 55.8 %collective-permute-start.2 = (bf16[256,1152]{1,0:T(8,128)(2,1)S(1)}, bf16[256,1152]{1,0:T(8,128)(2,1)S(1)}, u32[]{:S(2)}, u32[]{:S(2)}) collective-permute-start(bf16[256,1152]{1,0:T(8,128)(2,1)S(1)} %fusion.68), channel_id=1, source_target_pairs={{0,1},{1,2},{2,3},{3,4},{4,5},{5,6},{6,7},{7,8},{8,9},{9,10},{10,1... | collective-permute-start | bytes 1769480 | tf_op jit(solution)/shard_map/ppermute | solution.py:12
  123.3 0.4 fusion.64
  124.1 4.1 %collective-permute-start.12 = (bf16[256,1152]{1,0:T(8,128)(2,1)S(1)}, bf16[256,1152]{1,0:T(8,128)(2,1)S(1)}, u32[]{:S(2)}, u32[]{:S(2)}) collective-permute-start(bf16[256,1152]{1,0:T(8,128)(2,1)S(1)} %convolution_convert_fusion.2), channel_id=1, source_target_pairs={{0,511},{1,0},{2,1},{3,2},{4,3},{5,4},{6,5},{7,6},{8,7},{9,8},{10,... | collective-permute-start | bytes 1769480 | tf_op jit(solution)/shard_map/ppermute | solution.py:12
  128.2 1.9 collective-permute-start.13
  130.2 0.4 fusion.66
  131.0 57.3 %collective-permute-done.2 = bf16[256,1152]{1,0:T(8,128)(2,1)S(1)} collective-permute-done((bf16[256,1152]{1,0:T(8,128)(2,1)S(1)}, bf16[256,1152]{1,0:T(8,128)(2,1)S(1)}, u32[]{:S(2)}, u32[]{:S(2)}) %collective-permute-start.2) | collective-permute-done | bytes 589856 | tf_op jit(solution)/shard_map/ppermute | solution.py:12
  188.3 1.9 collective-permute-start.14
  190.2 0.4 fusion.63
  191.0 1.9 collective-permute-start.3
  192.9 0.4 fusion.65
  194.1 1.9 collective-permute-start.7
  196.0 0.4 fusion.67
  197.9 1.9 collective-permute-start.11
  199.8 57.9 %collective-permute-done.14 = bf16[256,1152]{1,0:T(8,128)(2,1)S(1)} collective-permute-done((bf16[256,1152]{1,0:T(8,128)(2,1)S(1)}, bf16[256,1152]{1,0:T(8,128)(2,1)S(1)}, u32[]{:S(2)}, u32[]{:S(2)}) %collective-permute-start.14) | collective-permute-done | bytes 589856 | tf_op jit(solution)/shard_map/ppermute | solution.py:12
  257.7 0.9 multiply_reduce_fusion
  258.6 1.3 subtract_divide_fusion
  259.9 26.1 %collective-permute-done.11 = bf16[256,1152]{1,0:T(8,128)(2,1)S(1)} collective-permute-done((bf16[256,1152]{1,0:T(8,128)(2,1)S(1)}, bf16[256,1152]{1,0:T(8,128)(2,1)S(1)}, u32[]{:S(2)}, u32[]{:S(2)}) %collective-permute-start.11) | collective-permute-done | bytes 589856 | tf_op jit(solution)/shard_map/ppermute | solution.py:12
  286.1 0.9 multiply_reduce_fusion.1
  286.9 1.3 subtract_divide_fusion.1
  (33 shorter events, 5.2 us)
Async XLA Ops:
  0.6 22.9 %copy-start.1 = (bf16[256,1152]{1,0:T(8,128)(2,1)S(1)}, bf16[256,1152]{1,0:T(8,128)(2,1)}, u32[]{:S(2)}) copy-start(bf16[256,1152]{1,0:T(8,128)(2,1)} %param.5) | copy-start | bytes 1769476
  0.6 53.7 %collective-permute-start.5 = (s32[256]{0:T(256)}, s32[256]{0:T(256)S(1)}, u32[]{:S(2)}, u32[]{:S(2)}) collective-permute-start(s32[256]{0:T(256)} %param.7), channel_id=1, source_target_pairs={{0,86},{1,87},{2,88},{3,89},{4,90},{5,91},{6,92},{7,93},{8,94},{9,... | collective-permute-start | bytes 3080 | tf_op jit(solution)/shard_map/ppermute | solution.py:12
  13.2 20.6 %collective-permute-start.1 = (s32[256]{0:T(256)}, s32[256]{0:T(256)S(1)}, u32[]{:S(2)}, u32[]{:S(2)}) collective-permute-start(s32[256]{0:T(256)} %param.7), channel_id=1, source_target_pairs={{0,1},{1,2},{2,3},{3,4},{4,5},{5,6},{6,7},{7,8},{8,9},{9,10},{10,1... | collective-permute-start | bytes 3080 | tf_op jit(solution)/shard_map/ppermute | solution.py:12
  19.7 13.0 %copy-start.2 = (s32[256]{0:T(256)S(1)}, s32[256]{0:T(256)}, u32[]{:S(2)}) copy-start(s32[256]{0:T(256)} %param.7) | copy-start | bytes 3076
  19.7 32.0 %collective-permute-start = (bf16[256,1152]{1,0:T(8,128)(2,1)S(1)}, bf16[256,1152]{1,0:T(8,128)(2,1)S(1)}, u32[]{:S(2)}, u32[]{:S(2)}) collective-permute-start(bf16[256,1152]{1,0:T(8,128)(2,1)S(1)} %fusion.69), channel_id=1, source_target_pairs={{0,1},{1,2},{2,3},{3,4},{4,5},{5,6},{6,7},{7,8},{8,9},{9,10},{10,1... | collective-permute-start | bytes 1769480 | tf_op jit(solution)/shard_map/ppermute | solution.py:12
  21.6 45.8 %collective-permute-start.4 = (bf16[256,1152]{1,0:T(8,128)(2,1)S(1)}, bf16[256,1152]{1,0:T(8,128)(2,1)S(1)}, u32[]{:S(2)}, u32[]{:S(2)}) collective-permute-start(bf16[256,1152]{1,0:T(8,128)(2,1)S(1)} %fusion.69), channel_id=1, source_target_pairs={{0,86},{1,87},{2,88},{3,89},{4,90},{5,91},{6,92},{7,93},{8,94},{9,... | collective-permute-start | bytes 1769480 | tf_op jit(solution)/shard_map/ppermute | solution.py:12
  24.0 167.0 %collective-permute-start.6 = (bf16[256,1152]{1,0:T(8,128)(2,1)S(1)}, bf16[256,1152]{1,0:T(8,128)(2,1)S(1)}, u32[]{:S(2)}, u32[]{:S(2)}) collective-permute-start(bf16[256,1152]{1,0:T(8,128)(2,1)S(1)} %fusion.68), channel_id=1, source_target_pairs={{0,86},{1,87},{2,88},{3,89},{4,90},{5,91},{6,92},{7,93},{8,94},{9,... | collective-permute-start | bytes 1769480 | tf_op jit(solution)/shard_map/ppermute | solution.py:12
  33.8 160.3 %collective-permute-start.10 = (bf16[256,1152]{1,0:T(8,128)(2,1)S(1)}, bf16[256,1152]{1,0:T(8,128)(2,1)S(1)}, u32[]{:S(2)}, u32[]{:S(2)}) collective-permute-start(bf16[256,1152]{1,0:T(8,128)(2,1)S(1)} %fusion.68), channel_id=1, source_target_pairs={{0,171},{1,172},{2,173},{3,174},{4,175},{5,176},{6,177},{7,178},{8... | collective-permute-start | bytes 1769480 | tf_op jit(solution)/shard_map/ppermute | solution.py:12
  51.7 76.6 %collective-permute-start.8 = (bf16[256,1152]{1,0:T(8,128)(2,1)S(1)}, bf16[256,1152]{1,0:T(8,128)(2,1)S(1)}, u32[]{:S(2)}, u32[]{:S(2)}) collective-permute-start(bf16[256,1152]{1,0:T(8,128)(2,1)S(1)} %fusion.69), channel_id=1, source_target_pairs={{0,171},{1,172},{2,173},{3,174},{4,175},{5,176},{6,177},{7,178},{8... | collective-permute-start | bytes 1769480 | tf_op jit(solution)/shard_map/ppermute | solution.py:12
  54.4 69.7 %collective-permute-start.9 = (s32[256]{0:T(256)S(1)}, s32[256]{0:T(256)S(1)}, u32[]{:S(2)}, u32[]{:S(2)}) collective-permute-start(s32[256]{0:T(256)S(1)} %copy-done.2), channel_id=1, source_target_pairs={{0,171},{1,172},{2,173},{3,174},{4,175},{5,176},{6,177},{7,178},{8... | collective-permute-start | bytes 3080 | tf_op jit(solution)/shard_map/ppermute | solution.py:12
  67.4 120.9 %collective-permute-start.2 = (bf16[256,1152]{1,0:T(8,128)(2,1)S(1)}, bf16[256,1152]{1,0:T(8,128)(2,1)S(1)}, u32[]{:S(2)}, u32[]{:S(2)}) collective-permute-start(bf16[256,1152]{1,0:T(8,128)(2,1)S(1)} %fusion.68), channel_id=1, source_target_pairs={{0,1},{1,2},{2,3},{3,4},{4,5},{5,6},{6,7},{7,8},{8,9},{9,10},{10,1... | collective-permute-start | bytes 1769480 | tf_op jit(solution)/shard_map/ppermute | solution.py:12
  124.1 73.8 %collective-permute-start.12 = (bf16[256,1152]{1,0:T(8,128)(2,1)S(1)}, bf16[256,1152]{1,0:T(8,128)(2,1)S(1)}, u32[]{:S(2)}, u32[]{:S(2)}) collective-permute-start(bf16[256,1152]{1,0:T(8,128)(2,1)S(1)} %convolution_convert_fusion.2), channel_id=1, source_target_pairs={{0,511},{1,0},{2,1},{3,2},{4,3},{5,4},{6,5},{7,6},{8,7},{9,8},{10,... | collective-permute-start | bytes 1769480 | tf_op jit(solution)/shard_map/ppermute | solution.py:12
  128.2 71.6 %collective-permute-start.13 = (bf16[256,1152]{1,0:T(8,128)(2,1)S(1)}, bf16[256,1152]{1,0:T(8,128)(2,1)S(1)}, u32[]{:S(2)}, u32[]{:S(2)}) collective-permute-start(bf16[256,1152]{1,0:T(8,128)(2,1)S(1)} %convolution_convert_fusion.1), channel_id=1, source_target_pairs={{0,426},{1,427},{2,428},{3,429},{4,430},{5,431},{6,432},{7,433},{8... | collective-permute-start | bytes 1769480 | tf_op jit(solution)/shard_map/ppermute | solution.py:12
  188.3 69.4 %collective-permute-start.14 = (bf16[256,1152]{1,0:T(8,128)(2,1)S(1)}, bf16[256,1152]{1,0:T(8,128)(2,1)S(1)}, u32[]{:S(2)}, u32[]{:S(2)}) collective-permute-start(bf16[256,1152]{1,0:T(8,128)(2,1)S(1)} %convolution_convert_fusion), channel_id=1, source_target_pairs={{0,341},{1,342},{2,343},{3,344},{4,345},{5,346},{6,347},{7,348},{8... | collective-permute-start | bytes 1769480 | tf_op jit(solution)/shard_map/ppermute | solution.py:12
  191.0 68.9 %collective-permute-start.3 = (bf16[256,1152]{1,0:T(8,128)(2,1)S(1)}, bf16[256,1152]{1,0:T(8,128)(2,1)S(1)}, u32[]{:S(2)}, u32[]{:S(2)}) collective-permute-start(bf16[256,1152]{1,0:T(8,128)(2,1)S(1)} %convolution_convert_fusion.5), channel_id=1, source_target_pairs={{0,511},{1,0},{2,1},{3,2},{4,3},{5,4},{6,5},{7,6},{8,7},{9,8},{10,... | collective-permute-start | bytes 1769480 | tf_op jit(solution)/shard_map/ppermute | solution.py:12
  194.1 65.8 %collective-permute-start.7 = (bf16[256,1152]{1,0:T(8,128)(2,1)S(1)}, bf16[256,1152]{1,0:T(8,128)(2,1)S(1)}, u32[]{:S(2)}, u32[]{:S(2)}) collective-permute-start(bf16[256,1152]{1,0:T(8,128)(2,1)S(1)} %convolution_convert_fusion.4), channel_id=1, source_target_pairs={{0,426},{1,427},{2,428},{3,429},{4,430},{5,431},{6,432},{7,433},{8... | collective-permute-start | bytes 1769480 | tf_op jit(solution)/shard_map/ppermute | solution.py:12
  197.5 60.2 %copy-start = (bf16[256,1152]{1,0:T(8,128)(2,1)S(1)}, bf16[256,1152]{1,0:T(8,128)(2,1)}, u32[]{:S(2)}) copy-start(bf16[256,1152]{1,0:T(8,128)(2,1)} %param.6) | copy-start | bytes 1769476
  197.9 88.1 %collective-permute-start.11 = (bf16[256,1152]{1,0:T(8,128)(2,1)S(1)}, bf16[256,1152]{1,0:T(8,128)(2,1)S(1)}, u32[]{:S(2)}, u32[]{:S(2)}) collective-permute-start(bf16[256,1152]{1,0:T(8,128)(2,1)S(1)} %convolution_convert_fusion.3), channel_id=1, source_target_pairs={{0,341},{1,342},{2,343},{3,344},{4,345},{5,346},{6,347},{7,348},{8... | collective-permute-start | bytes 1769480 | tf_op jit(solution)/shard_map/ppermute | solution.py:12
where the time goes:
time: 289 us; the launch traced here: 288 us
  waiting for transfers between devices  166 us (57%)
  starting transfers between devices  106 us (37%)
  matrix products  9 us (3%)
  other arithmetic  5.58 us (2%)
    ppermute x15, waiting for transfers between devices, from_behind(): return lax.ppermute(value, axis, pairs)  166 us
    ppermute x15, starting transfers between devices, from_behind(): return lax.ppermute(value, axis, pairs)  106 us
    dot_general x14, matrix products, product(): return jnp.dot(left_rows, right_rows, preferred_element_type=jnp.float32)  6.13 us
  transfers between devices with their start and end apart: 15, of which 5 were waited for; matrix products, arithmetic and copies ran while one was open for 4% of the time, Pallas kernels for 0%

commit v1 on v0

v1 whole, which is shorter than its diff:
```python
import jax
import jax.numpy as jnp
from jax import lax
from jax.experimental import pallas as pl
from jax.experimental.pallas import tpu as pltpu
from jax.sharding import PartitionSpec as P

MESH = pl.DeviceIdType.MESH
NDEV = 512
ROWS = 256
D = 1152
CHUNKS = 16
SIZE = 2 * ROWS // CHUNKS
SKEW = 3
HALF = 128
LEGS = ("near", "fix", "fj", "fk", "A", "B", "sk", "sl", "sm", "C", "D")
NEXT = {"near": ("fj", "fix"), "sk": ("sl",), "fj": ("fk",), "sl": ("sm", "D"), "fk": ("A", "B"), "sm": ("C",)}
DELAY = {"near": 0, "sk": 0, "fj": 1, "sl": 1, "fk": 2, "sm": 2, "A": 3, "B": 3, "C": 3, "D": 3}
ORDER = ("A", "B", "C", "D", "fk", "sm", "fj", "sl", "near", "sk")


def coords(i):
    return i // 128, (i // 16) % 8, (i // 2) % 8, i % 2


def index(x, y, z, core):
    return (((x + 8) % 4 * 8 + (y + 16) % 8) * 8 + (z + 16) % 8) * 2 + core


def wrap(i):
    return (i + 2 * NDEV) % NDEV


def side(core):
    return 2 * core - 1


def y_steps(z_start, d):
    return d * 5 + (z_start + 3 * d + 8) // 8 - 1


def along_z(i, n):
    x, y, z, core = coords(i)
    return index(x, y, z + n * side(core), core)


def other_z(i, n):
    x, y, z, core = coords(i)
    return index(x, y, z + n * side(core), 1 - core)


def along_y(i, z_start, d, sign):
    x, y, z, core = coords(i)
    return index(x, y + sign * y_steps(z_start, d), z, core)


def f_z_start(i):
    _, _, z, core = coords(i)
    return (z - 3 * side(core) + 16) % 8


def f_y(i, sign):
    return along_y(i, f_z_start(i), side(i % 2), sign)


def f_hold(owner):
    return f_y(along_z(owner, 3), 1)


def f_owner(i):
    return along_z(f_y(i, -1), -3)


def s_y(i, sign):
    return along_y(i, (i // 2) % 8, -side(i % 2), sign)


def s_hold(owner, n):
    return along_z(s_y(owner, 1), -n)


def s_owner(i, n):
    return s_y(along_z(i, n), -1)


def kernel(scale_ref, bias_ref, ids_ref, img_ref, txt_ref, out_img, out_txt, near, fj, fk, sk, sl, sm, far, part, own,
           hat, keys, coeff, ids, far_ids, send_sem, recv_sem, part_sem, id_sem, own_sem):
    me = lax.axis_index("dp")
    _, _, z, core = coords(me)
    s = side(core)
    barrier = pltpu.get_barrier_semaphore()

    f_own, s_own2, s_own3 = f_owner(me), s_owner(me, 2), s_owner(me, 3)
    target = {
        "near": other_z(me, 1), "fix": wrap(me - 16 * s), "fj": other_z(me, -2), "fk": f_y(me, 1),
        "A": wrap(f_own + 86 * s), "B": wrap(f_own - 171 * s),
        "sk": s_y(me, 1), "sl": along_z(me, -2), "sm": along_z(me, -1),
        "C": wrap(s_own3 - 86 * s), "D": wrap(s_own2 + 171 * s),
    }
    source = {
        "near": other_z(me, 1), "fix": wrap(me + 16 * s), "fj": other_z(me, -2), "fk": f_y(me, -1),
        "A": f_hold(wrap(me - 86 * s)), "B": f_hold(wrap(me - 171 * s)),
        "sk": s_y(me, -1), "sl": along_z(me, 2), "sm": along_z(me, 1),
        "C": s_hold(wrap(me + 86 * s), 3), "D": s_hold(wrap(me + 171 * s), 2),
    }
    partner = wrap(me - s)
    id_to = [partner, wrap(me + s), wrap(me + 86 * s), wrap(me - 171 * s), wrap(me - 86 * s), wrap(me + 171 * s)]
    id_from = [partner, wrap(me + s), wrap(me - 86 * s), wrap(me - 171 * s), wrap(me + 86 * s), wrap(me + 171 * s)]
    only = {"fix": z == 7 * core, "A": target["A"] != me, "C": target["C"] != me}

    own_copies = [pltpu.make_async_copy(r, own.at[a], own_sem.at[a]) for a, r in ((0, img_ref), (1, txt_ref))]
    for copy in own_copies:
        copy.start()

    def signal(device):
        pl.semaphore_signal(barrier, inc=1, device_id=(device,), device_id_type=MESH)

    always = [leg for leg in LEGS if leg not in only]
    for leg in always:
        signal(source[leg])
    for device in id_from:
        signal(device)
    for leg, where in only.items():
        pl.when(where)(lambda leg=leg: signal(source[leg]))
    pl.semaphore_wait(barrier, len(always) + len(id_from) + sum(jnp.where(where, 1, 0) for where in only.values()))

    def own_rows(i):
        first = i * SIZE
        return txt_ref.at[pl.ds(first, SIZE)] if first < ROWS else img_ref.at[pl.ds(first - ROWS, SIZE)]

    def place(leg, i):
        rows = pl.ds(i * SIZE, SIZE)
        if leg in ("near", "fix"):
            return near.at[int(leg == "fix"), rows]
        if leg in "ABCD":
            per = HALF // SIZE
            return far.at[i // per, pl.ds("ABCD".index(leg) * HALF + i % per * SIZE, SIZE)]
        return {"fj": fj, "fk": fk, "sk": sk, "sl": sl, "sm": sm}[leg].at[rows]

    came_by = {out: leg for leg, outs in NEXT.items() for out in outs}

    def start_of(leg, i):
        return place(came_by[leg], i) if leg in came_by else own_rows(i)

    def remote(leg, i):
        j = LEGS.index(leg)
        return pltpu.make_async_remote_copy(
            src_ref=start_of(leg, i), dst_ref=place(leg, i), send_sem=send_sem.at[j, i], recv_sem=recv_sem.at[j, i],
            device_id=(target[leg],), device_id_type=MESH)

    def send(leg, i):
        if leg in only:
            pl.when(only[leg])(lambda: remote(leg, i).start())
            if leg != "fix":
                pl.when(jnp.logical_not(only[leg]))(lambda: pltpu.make_async_copy(
                    start_of(leg, i), place(leg, i), recv_sem.at[LEGS.index(leg), i]).start())
        else:
            remote(leg, i).start()

    def whole(a):
        ref = (txt_ref, img_ref)[a]
        return pltpu.make_async_remote_copy(
            src_ref=ref, dst_ref=part.at[pl.ds(a * ROWS, ROWS)], send_sem=part_sem.at[a], recv_sem=part_sem.at[2 + a],
            device_id=(partner,), device_id_type=MESH)

    def send_ids(j):
        return pltpu.make_async_remote_copy(
            src_ref=ids, dst_ref=far_ids.at[j], send_sem=id_sem.at[j], recv_sem=id_sem.at[6 + j],
            device_id=(id_to[j],), device_id_type=MESH)

    for i in range(CHUNKS):
        send("near", i)
        send("sk", i)
    ids[...] = jnp.broadcast_to(ids_ref[...], (8, ROWS))
    for j in range(6):
        send_ids(j).start()
    for a in range(2):
        whole(a).start()

    scale, bias = scale_ref[0], bias_ref[0]
    diagonal = lax.broadcasted_iota(jnp.int32, (ROWS, ROWS), 0) == lax.broadcasted_iota(jnp.int32, (ROWS, ROWS), 1)
    my_ids = jnp.sum(jnp.where(diagonal, jnp.broadcast_to(ids_ref[...], (ROWS, ROWS)), 0), axis=1, keepdims=True)

    def normalize(read, write, rows):
        def body(i, carry):
            first = pl.multiple_of(i * 32, 32)
            values = read(first).astype(jnp.float32)
            norms = jnp.sqrt(jnp.sum(values * values, axis=1, keepdims=True) + 1e-6)
            write(first, (values * (1.0 / norms)).astype(jnp.bfloat16))
            return carry
        lax.fori_loop(0, rows // 32, body, 0)

    def gain(a, key_rows, key_ids, out, first=False):
        count = key_rows.shape[0]
        scores = lax.dot_general(hat[a], key_rows[...], (((1,), (1,)), ((), ())), preferred_element_type=jnp.float32)
        positive = (my_ids == key_ids).astype(jnp.float32)
        coeff[:, pl.ds(0, count)] = (scale * (jax.nn.sigmoid(scale * scores + bias) - positive)).astype(jnp.bfloat16)
        term = jnp.dot(coeff[:, pl.ds(0, count)], key_rows[...], preferred_element_type=jnp.float32)
        if first:
            out[...] = term
        else:
            out[...] += term

    def keys_from(read, rows):
        def write(first, value):
            keys[pl.ds(first, 32)] = value
        normalize(read, write, rows)
        return keys.at[pl.ds(0, rows)]

    outs = (out_img, out_txt)

    def own_step():
        for a in range(2):
            own_copies[a].wait()
            def write(first, value):
                hat[a, pl.ds(first, 32)] = value
            normalize(lambda first: own[a, pl.ds(first, 32)], write, ROWS)
        for a in range(2):
            gain(a, hat.at[1 - a], ids_ref[...], outs[a], first=True)

    def partner_step(a):
        whole(a).wait_recv()
        rows = keys_from(lambda first: part[pl.ds(a * ROWS + first, 32)], ROWS)
        gain(a, rows, far_ids[0, pl.ds(0, 1)], outs[a])

    def near_step(a):
        for i in range(a * CHUNKS // 2, (a + 1) * CHUNKS // 2):
            pl.when(only["fix"])(lambda: remote("fix", i).wait_recv())
        slot = jnp.where(only["fix"], 1, 0)
        rows = keys_from(lambda first: near[slot, pl.ds(a * ROWS + first, 32)], ROWS)
        gain(a, rows, far_ids[1, pl.ds(0, 1)], outs[a])

    def far_step(part_of):
        a, half = part_of // 2, part_of % 2
        rows = keys_from(lambda first: far[part_of, pl.ds(first, 32)], 4 * HALF)
        lanes = pl.ds(half * HALF, HALF)
        key_ids = jnp.concatenate([far_ids[j, pl.ds(0, 1), lanes] for j in range(2, 6)], axis=1)
        gain(a, rows, key_ids, outs[a])

    todo = {1: own_step, 2: lambda: [send_ids(j).wait_recv() for j in range(6)] and partner_step(0),
            3: lambda: partner_step(1), 9: lambda: near_step(0), 17: lambda: near_step(1)}
    for t in range(CHUNKS + 3 * SKEW):
        for leg in ORDER:
            i = t - DELAY[leg] * SKEW
            if 0 <= i < CHUNKS:
                remote(leg, i).wait_recv()
                for out in NEXT.get(leg, ()):
                    send(out, i)
        if t in todo:
            todo[t]()
        i = t - 3 * SKEW
        if 0 <= i and (i + 1) % (HALF // SIZE) == 0:
            far_step(i // (HALF // SIZE))

    for a, ref, out in ((0, img_ref, out_img), (1, txt_ref, out_txt)):
        def body(i, carry):
            rows = pl.ds(pl.multiple_of(i * 32, 32), 32)
            values = own[a, rows].astype(jnp.float32)
            inverse = 1.0 / jnp.sqrt(jnp.sum(values * values, axis=1, keepdims=True) + 1e-6)
            unit = values * inverse
            grad = out[rows]
            out[rows] = (grad - unit * jnp.sum(unit * grad, axis=1, keepdims=True)) * inverse
            return carry
        lax.fori_loop(0, ROWS // 32, body, 0)

    for i in range(CHUNKS):
        for leg in LEGS:
            if leg in only:
                pl.when(only[leg])(lambda: remote(leg, i).wait_send())
            else:
                remote(leg, i).wait_send()
    for a in range(2):
        whole(a).wait_send()
    for j in range(6):
        send_ids(j).wait_send()


def per_device(image_emb, text_emb, pair_id, logit_scale, logit_bias):
    def rows(*shape):
        return pltpu.VMEM(shape, jnp.bfloat16)
    smem, vmem = (pl.BlockSpec(memory_space=m) for m in (pltpu.SMEM, pltpu.VMEM))
    grad = jax.ShapeDtypeStruct((ROWS, D), jnp.float32)
    return pl.pallas_call(
        kernel,
        out_shape=(grad, grad),
        in_specs=[smem, smem, vmem, pl.BlockSpec(memory_space=pl.ANY), pl.BlockSpec(memory_space=pl.ANY)],
        out_specs=(vmem, vmem),
        scratch_shapes=[
            rows(2, 2 * ROWS, D), *[rows(2 * ROWS, D)] * 5, rows(4, 4 * HALF, D), rows(2 * ROWS, D), rows(2, ROWS, D),
            rows(2, ROWS, D), rows(4 * HALF, D), rows(ROWS, 4 * HALF),
            pltpu.VMEM((8, ROWS), jnp.int32), pltpu.VMEM((6, 8, ROWS), jnp.int32),
            pltpu.SemaphoreType.DMA((len(LEGS), CHUNKS)), pltpu.SemaphoreType.DMA((len(LEGS), CHUNKS)),
            pltpu.SemaphoreType.DMA((4,)), pltpu.SemaphoreType.DMA((12,)), pltpu.SemaphoreType.DMA((2,)),
        ],
        compiler_params=pltpu.CompilerParams(collective_id=0, has_side_effects=True, vmem_limit_bytes=48 * 2**20),
        cost_estimate=pl.CostEstimate(flops=28 * ROWS * ROWS * D * 2, bytes_accessed=6 * ROWS * D * 4, transcendentals=14 * ROWS * ROWS),
    )(logit_scale, logit_bias, pair_id.reshape(1, ROWS), image_emb, text_emb)


def solution(mesh):
    in_specs = (P("dp", None), P("dp", None), P("dp"), P(), P())
    out_specs = (P("dp", None), P("dp", None))
    return jax.shard_map(
        per_device, mesh=mesh, in_specs=in_specs, out_specs=out_specs, check_vma=False
    )
```

time: 289 us -> 146 us (0.51)
  the two profiles are of different devices: /device:TPU:131 before, /device:TPU:1 now
where the time goes in v1:
time: 146 us
  Pallas kernels  139 us (95%)
  local copies, waits for them, and re-layouts  4.83 us (3%)
  between operations  1.94 us (1%)
    pallas_call x1, Pallas kernels, per_device(): pl.pallas_call(kernel, out_shape=(grad, grad), in_specs=[smem, smem, vmem...  139 us
    unnamed x8, local copies, waits for them, and re-layouts  4.83 us

profile of v1, /device:TPU:1, one launch (start us, length us, event | category | flops | bytes accessed | tf_op | source)
XLA Modules:
  0.0 145.7 jit_solution(14103607004210532135)
XLA Ops:
  1.9 0.0 copy-start
  1.9 1.1 copy-done
  3.0 0.0 copy-start.1
  3.0 1.1 copy-done.1
  4.1 0.0 copy-start.2
  4.1 0.7 copy-done.2
  4.7 138.9 %shard_map.68 = (f32[256,1152]{1,0:T(8,128)S(1)}, f32[256,1152]{1,0:T(8,128)S(1)}) custom-call(f32[1]{0:T(128)S(6)} %copy.9.scale_ref, f32[1]{0:T(128)S(6)} %copy.10.bias_ref, s32[1,256]{1,0:T(1,128)S(1)} %bitcast.1, bf16[256,1152]{1,0:T(8,128)(2,1)S(1)} %copy-done, bf16[256,1152]{1,0:T(8,128)(2,1)S(1)} %copy-done.1), custom_call_target="tpu_custom_call" | custom-call | flops 4227858432 | bytes 7077888 | tf_op jit(solution)/shard_map/pallas_call | solution.py:283
  143.7 1.0 copy.11
  144.7 1.0 copy.12
Async XLA Ops:
  1.9 1.1 copy-start
  3.0 1.1 copy-start.1
  4.1 0.7 copy-start.2

commit v2 on v1

v2 whole, which is shorter than its diff:
```python
import jax
import jax.numpy as jnp
from jax import lax
from jax.experimental import pallas as pl
from jax.experimental.pallas import tpu as pltpu
from jax.sharding import PartitionSpec as P

MESH = pl.DeviceIdType.MESH
NDEV = 512
ROWS = 256
D = 1152
CHUNKS = 16
SIZE = 2 * ROWS // CHUNKS
HALF = 128
NORM_ROWS = 64
PROJECT_ROWS = 64
VMEM_LIMIT = 56 * 2**20
LEGS = ("near", "fix", "fj", "fk", "A", "B", "sk", "sl", "sm", "C", "D")
NEXT = {"near": ("fj", "fix"), "sk": ("sl",), "fj": ("fk",), "sl": ("sm", "D"), "fk": ("A", "B"), "sm": ("C",)}
DELAY = {"near": 0, "sk": 0, "fj": 3, "sl": 3, "fk": 6, "sm": 6, "A": 9, "B": 9, "C": 9, "D": 9}
ORDER = ("A", "B", "C", "D", "fk", "sm", "fj", "sl", "near", "sk")
CLOSE_AT = (10, 18)


def coords(i):
    return i // 128, (i // 16) % 8, (i // 2) % 8, i % 2


def index(x, y, z, core):
    return (((x + 8) % 4 * 8 + (y + 16) % 8) * 8 + (z + 16) % 8) * 2 + core


def wrap(i):
    return (i + 2 * NDEV) % NDEV


def side(core):
    return 2 * core - 1


def y_steps(z_start, d):
    return d * 5 + (z_start + 3 * d + 8) // 8 - 1


def along_z(i, n):
    x, y, z, core = coords(i)
    return index(x, y, z + n * side(core), core)


def other_z(i, n):
    x, y, z, core = coords(i)
    return index(x, y, z + n * side(core), 1 - core)


def along_y(i, z_start, d, sign):
    x, y, z, core = coords(i)
    return index(x, y + sign * y_steps(z_start, d), z, core)


def f_z_start(i):
    _, _, z, core = coords(i)
    return (z - 3 * side(core) + 16) % 8


def f_y(i, sign):
    return along_y(i, f_z_start(i), side(i % 2), sign)


def f_hold(owner):
    return f_y(along_z(owner, 3), 1)


def f_owner(i):
    return along_z(f_y(i, -1), -3)


def s_y(i, sign):
    return along_y(i, (i // 2) % 8, -side(i % 2), sign)


def s_hold(owner, n):
    return along_z(s_y(owner, 1), -n)


def s_owner(i, n):
    return s_y(along_z(i, n), -1)


def kernel(scale_ref, bias_ref, ids_ref, img_ref, txt_ref, out_img, out_txt, close, fj, sk, sl, far, raw, coeff, ids,
           far_ids, send_sem, recv_sem, part_sem, id_sem, own_sem):
    me = lax.axis_index("dp")
    _, _, z, core = coords(me)
    s = side(core)
    barrier = pltpu.get_barrier_semaphore()

    own_copies = [pltpu.make_async_copy(r, raw.at[a], own_sem.at[a]) for a, r in ((0, txt_ref), (1, img_ref))]
    for copy in own_copies:
        copy.start()

    def is_edge(z, core):
        return z == 7 * core

    f_own, s_own2, s_own3 = f_owner(me), s_owner(me, 2), s_owner(me, 3)
    target = {
        "near": other_z(me, 1), "fix": wrap(me - 16 * s), "fj": other_z(me, -2), "fk": f_y(me, 1),
        "A": wrap(f_own + 86 * s), "B": wrap(f_own - 171 * s),
        "sk": s_y(me, 1), "sl": along_z(me, -2), "sm": along_z(me, -1),
        "C": wrap(s_own3 - 86 * s), "D": wrap(s_own2 + 171 * s),
    }
    source = {
        "near": other_z(me, 1), "fix": wrap(me + 16 * s), "fj": other_z(me, -2), "fk": f_y(me, -1),
        "A": f_hold(wrap(me - 86 * s)), "B": f_hold(wrap(me - 171 * s)),
        "sk": s_y(me, -1), "sl": along_z(me, 2), "sm": along_z(me, 1),
        "C": s_hold(wrap(me + 86 * s), 3), "D": s_hold(wrap(me + 171 * s), 2),
    }
    partner = wrap(me - s)
    id_to = [partner, wrap(me + s), wrap(me + 86 * s), wrap(me - 171 * s), wrap(me - 86 * s), wrap(me + 171 * s)]
    id_from = [partner, wrap(me + s), wrap(me - 86 * s), wrap(me - 171 * s), wrap(me + 86 * s), wrap(me + 171 * s)]
    only = {"fix": is_edge(z, core), "A": target["A"] != me, "C": target["C"] != me}
    passes = {leg: jnp.where(where, 1, 0) for leg, where in only.items()}

    def signal(device):
        pl.semaphore_signal(barrier, inc=1, device_id=(device,), device_id_type=MESH)

    always = [leg for leg in LEGS if leg not in only]
    for leg in always:
        signal(source[leg])
    for device in id_from:
        signal(device)
    for leg, where in only.items():
        pl.when(where)(lambda leg=leg: signal(source[leg]))

    for a in range(2):
        own_copies[a].wait()

        def body(i, carry):
            first = pl.multiple_of(i * NORM_ROWS, NORM_ROWS)
            values = raw[a, pl.ds(first, NORM_ROWS)].astype(jnp.float32)
            norms = jnp.sqrt(jnp.sum(values * values, axis=1, keepdims=True) + 1e-6)
            close[0, pl.ds(a * ROWS + first, NORM_ROWS)] = (values * (1.0 / norms)).astype(jnp.bfloat16)
            return carry
        lax.fori_loop(0, ROWS // NORM_ROWS, body, 0)
    ids[...] = jnp.broadcast_to(ids_ref[...], (8, ROWS))

    pl.semaphore_wait(barrier, len(always) + len(id_from) + sum(passes.values()))

    _, _, next_z, next_core = coords(target["near"])
    near_slot = 2 + passes["fix"]
    near_slot_there = 2 + jnp.where(is_edge(next_z, next_core), 1, 0)
    f_next, s_next = target["fk"], target["sm"]
    a_there = jnp.where(wrap(f_owner(f_next) + 86 * s) != f_next, 4, 0)
    c_there = jnp.where(wrap(s_owner(s_next, 3) - 86 * s) != s_next, 5, 2)
    a_here, c_here = 4 * passes["A"], 2 + 3 * passes["C"]

    def far_rows(slot, i):
        per = HALF // SIZE
        return far.at[i // per, pl.ds(pl.multiple_of(slot * HALF + i % per * SIZE, SIZE), SIZE)]

    def to(leg, i):
        rows = pl.ds(i * SIZE, SIZE)
        if leg == "near":
            return close.at[near_slot_there, rows]
        if leg == "fix":
            return close.at[2, rows]
        if leg == "fk":
            return far_rows(a_there, i)
        if leg == "sm":
            return far_rows(c_there, i)
        if leg in "ABCD":
            return far_rows("ABCD".index(leg), i)
        return {"fj": fj, "sk": sk, "sl": sl}[leg].at[rows]

    def at(leg, i):
        if leg == "near":
            return close.at[near_slot, pl.ds(i * SIZE, SIZE)]
        if leg == "fk":
            return far_rows(a_here, i)
        if leg == "sm":
            return far_rows(c_here, i)
        return to(leg, i)

    came_by = {out: leg for leg, outs in NEXT.items() for out in outs}

    def remote(leg, i):
        j = LEGS.index(leg)
        return pltpu.make_async_remote_copy(
            src_ref=at(came_by[leg], i) if leg in came_by else close.at[0, pl.ds(i * SIZE, SIZE)],
            dst_ref=to(leg, i), send_sem=send_sem.at[j, i], recv_sem=recv_sem.at[j, i],
            device_id=(target[leg],), device_id_type=MESH)

    def do(leg, i, what):
        if leg in only:
            pl.when(only[leg])(lambda: getattr(remote(leg, i), what)())
        else:
            getattr(remote(leg, i), what)()

    def whole():
        return pltpu.make_async_remote_copy(
            src_ref=close.at[0], dst_ref=close.at[1], send_sem=part_sem.at[0], recv_sem=part_sem.at[1],
            device_id=(partner,), device_id_type=MESH)

    def send_ids(j):
        return pltpu.make_async_remote_copy(
            src_ref=ids, dst_ref=far_ids.at[j], send_sem=id_sem.at[j], recv_sem=id_sem.at[6 + j],
            device_id=(id_to[j],), device_id_type=MESH)

    for i in range(CHUNKS):
        do("near", i, "start")
        do("sk", i, "start")
    for j in range(6):
        send_ids(j).start()
    whole().start()

    scale, bias = scale_ref[0], bias_ref[0]
    diagonal = lax.broadcasted_iota(jnp.int32, (ROWS, ROWS), 0) == lax.broadcasted_iota(jnp.int32, (ROWS, ROWS), 1)
    my_ids = jnp.sum(jnp.where(diagonal, jnp.broadcast_to(ids_ref[...], (ROWS, ROWS)), 0), axis=1, keepdims=True)

    outs = (out_img, out_txt)

    def gain(a, key_rows, key_ids, first=False):
        scores = lax.dot_general(close[0, pl.ds((1 - a) * ROWS, ROWS)], key_rows, (((1,), (1,)), ((), ())),
                                 preferred_element_type=jnp.float32)
        positive = (my_ids == key_ids).astype(jnp.float32)
        count = key_rows.shape[0]
        coeff[:, pl.ds(0, count)] = (scale * (jax.nn.sigmoid(scale * scores + bias) - positive)).astype(jnp.bfloat16)
        term = jnp.dot(coeff[:, pl.ds(0, count)], key_rows, preferred_element_type=jnp.float32)
        if first:
            outs[a][...] = term
        else:
            outs[a][...] += term

    def close_step(a):
        if a == 0:
            whole().wait_recv()
            for j in range(6):
                send_ids(j).wait_recv()
        for i in range(a * CHUNKS // 2, (a + 1) * CHUNKS // 2):
            do("fix", i, "wait_recv")
        key_ids = jnp.concatenate([ids_ref[...], far_ids[0, pl.ds(0, 1)], far_ids[1, pl.ds(0, 1)]], axis=1)
        gain(a, close[pl.ds(0, 3), pl.ds(a * ROWS, ROWS)].reshape(3 * ROWS, D), key_ids, first=True)

    def far_step(part_of):
        a, half = part_of // 2, part_of % 2
        lanes = pl.ds(half * HALF, HALF)
        key_ids = jnp.concatenate([far_ids[j, pl.ds(0, 1), lanes] for j in range(2, 6)], axis=1)
        gain(a, far[part_of, pl.ds(0, 4 * HALF)], key_ids)

    for t in range(CHUNKS + max(DELAY.values())):
        for leg in ORDER:
            i = t - DELAY[leg]
            if 0 <= i < CHUNKS:
                do(leg, i, "wait_recv")
                for out in NEXT.get(leg, ()):
                    do(out, i, "start")
        if t in CLOSE_AT:
            close_step(CLOSE_AT.index(t))
        i = t - max(DELAY.values())
        if 0 <= i < CHUNKS - 1:
            for leg in LEGS:
                do(leg, i, "wait_send")
        if 0 <= i and (i + 1) % (HALF // SIZE) == 0:
            far_step(i // (HALF // SIZE))

    for leg in LEGS:
        do(leg, CHUNKS - 1, "wait_send")
    whole().wait_send()
    for j in range(6):
        send_ids(j).wait_send()


def project(grad_img, grad_txt, img, txt, out_img, out_txt, grads, raw, result, sem):
    pieces = [(a, pl.ds(i * PROJECT_ROWS, PROJECT_ROWS), i) for i in range(ROWS // PROJECT_ROWS) for a in range(2)]

    refs = ((grad_img, img, out_img), (grad_txt, txt, out_txt))

    def load_grad(a, rows, i):
        return pltpu.make_async_copy(refs[a][0].at[rows], grads.at[a, rows], sem.at[0, a, i])

    def load_emb(a, rows, i):
        return pltpu.make_async_copy(refs[a][1].at[rows], raw.at[a, rows], sem.at[1, a, i])

    def store(a, rows, i):
        return pltpu.make_async_copy(result.at[a, rows], refs[a][2].at[rows], sem.at[2, a, i])

    for piece in pieces:
        load_grad(*piece).start()
        load_emb(*piece).start()
    for a, rows, i in pieces:
        load_grad(a, rows, i).wait()
        load_emb(a, rows, i).wait()
        values, grad = raw[a, rows].astype(jnp.float32), grads[a, rows]
        inverse = 1.0 / jnp.sqrt(jnp.sum(values * values, axis=1, keepdims=True) + 1e-6)
        along = jnp.sum(values * grad, axis=1, keepdims=True) * (inverse * inverse)
        result[a, rows] = (grad - values * along) * inverse
        store(a, rows, i).start()
    for piece in pieces:
        store(*piece).wait()


def per_device(image_emb, text_emb, pair_id, logit_scale, logit_bias):
    def rows(*shape):
        return pltpu.VMEM(shape, jnp.bfloat16)
    smem, vmem = (pl.BlockSpec(memory_space=m) for m in (pltpu.SMEM, pltpu.VMEM))
    hbm = pl.BlockSpec(memory_space=pltpu.HBM)
    grad = jax.ShapeDtypeStruct((ROWS, D), jnp.float32)
    sums = pl.pallas_call(
        kernel,
        out_shape=(grad, grad),
        in_specs=[smem, smem, vmem, hbm, hbm],
        out_specs=(vmem, vmem),
        scratch_shapes=[
            rows(4, 2 * ROWS, D), *[rows(2 * ROWS, D)] * 3, rows(4, 6 * HALF, D), rows(2, ROWS, D), rows(ROWS, 3 * ROWS),
            pltpu.VMEM((8, ROWS), jnp.int32), pltpu.VMEM((6, 8, ROWS), jnp.int32),
            pltpu.SemaphoreType.DMA((len(LEGS), CHUNKS)), pltpu.SemaphoreType.DMA((len(LEGS), CHUNKS)),
            pltpu.SemaphoreType.DMA((2,)), pltpu.SemaphoreType.DMA((12,)), pltpu.SemaphoreType.DMA((2,)),
        ],
        compiler_params=pltpu.CompilerParams(collective_id=0, has_side_effects=True, vmem_limit_bytes=VMEM_LIMIT),
        cost_estimate=pl.CostEstimate(flops=28 * ROWS * ROWS * D * 2, bytes_accessed=6 * ROWS * D * 4, transcendentals=14 * ROWS * ROWS),
    )(logit_scale, logit_bias, pair_id.reshape(1, ROWS), image_emb, text_emb)
    return pl.pallas_call(
        project, out_shape=(grad, grad), in_specs=[hbm] * 4, out_specs=(hbm, hbm),
        scratch_shapes=[pltpu.VMEM((2, ROWS, D), jnp.float32), rows(2, ROWS, D), pltpu.VMEM((2, ROWS, D), jnp.float32),
                        pltpu.SemaphoreType.DMA((3, 2, ROWS // PROJECT_ROWS))],
        compiler_params=pltpu.CompilerParams(vmem_limit_bytes=VMEM_LIMIT),
        cost_estimate=pl.CostEstimate(flops=16 * ROWS * D, bytes_accessed=20 * ROWS * D, transcendentals=0),
    )(*sums, image_emb, text_emb)


def solution(mesh):
    in_specs = (P("dp", None), P("dp", None), P("dp"), P(), P())
    out_specs = (P("dp", None), P("dp", None))
    return jax.shard_map(
        per_device, mesh=mesh, in_specs=in_specs, out_specs=out_specs, check_vma=False
    )
```

time: 146 us -> 127 us (0.87)
  Pallas kernels: 139 us -> 125 us
  local copies, waits for them, and re-layouts: 4.83 us -> 0 us
    pallas_call x1, Pallas kernels: 139 us -> 122 us  [per_device(): pl.pallas_call(kernel, out_shape=(grad, grad), in_specs=[smem, smem, vmem...]
    unnamed x8 -> x0, local copies, waits for them, and re-layouts: 4.83 us -> none
    pallas_call x0 -> x1, Pallas kernels: none -> 3.15 us  [per_device(): pl.pallas_call(project, out_shape=(grad, grad), in_specs=[hbm] * 4, out_s...]
where the time goes in v2:
time: 127 us
  Pallas kernels  125 us (98%)
  between operations  1.93 us (2%)
    pallas_call x1, Pallas kernels, per_device(): pl.pallas_call(kernel, out_shape=(grad, grad), in_specs=[smem, smem, vmem...  122 us
    pallas_call x1, Pallas kernels, per_device(): pl.pallas_call(project, out_shape=(grad, grad), in_specs=[hbm] * 4, out_s...  3.15 us

profile of v2, /device:TPU:1, one launch (start us, length us, event | category | flops | bytes accessed | tf_op | source)
XLA Modules:
  0.0 126.7 jit_solution(15134105701335849656)
XLA Ops:
  1.9 121.6 %shard_map.68 = (f32[256,1152]{1,0:T(8,128)}, f32[256,1152]{1,0:T(8,128)}) custom-call(f32[1]{0:T(128)S(6)} %copy.7.scale_ref, f32[1]{0:T(128)S(6)} %copy.8.bias_ref, s32[1,256]{1,0:T(1,128)} %bitcast.1, bf16[256,1152]{1,0:T(8,128)(2,1)} %img.1, bf16[256,1152]{1,0:T(8,128)(2,1)} %txt.1), custom_call_target="tpu_custom_call" | custom-call | flops 4227858432 | bytes 7077888 | tf_op jit(solution)/shard_map/pallas_call | solution.py:306
  123.6 3.2 %shard_map.69 = (f32[256,1152]{1,0:T(8,128)}, f32[256,1152]{1,0:T(8,128)}) custom-call(f32[256,1152]{1,0:T(8,128)} %get-tuple-element.4.grad_img, f32[256,1152]{1,0:T(8,128)} %get-tuple-element.5.grad_txt, bf16[256,1152]{1,0:T(8,128)(2,1)} %img.1, bf16[256,1152]{1,0:T(8,128)(2,1)} %txt.1), custom_call_target="tpu_custom_call" | custom-call | flops 4718592 | bytes 5898240 | tf_op jit(solution)/shard_map/pallas_call | solution.py:320

commit v3 on v2

--- a/solution.py
+++ b/solution.py
@@ -15,11 +15,12 @@
 NORM_ROWS = 64
 PROJECT_ROWS = 64
 VMEM_LIMIT = 56 * 2**20
-LEGS = ("near", "fix", "fj", "fk", "A", "B", "sk", "sl", "sm", "C", "D")
+LEGS = ("near", "fix", "fj", "fk", "A", "B", "sk", "sl", "sm", "C", "D", "part")
 NEXT = {"near": ("fj", "fix"), "sk": ("sl",), "fj": ("fk",), "sl": ("sm", "D"), "fk": ("A", "B"), "sm": ("C",)}
 DELAY = {"near": 0, "sk": 0, "fj": 3, "sl": 3, "fk": 6, "sm": 6, "A": 9, "B": 9, "C": 9, "D": 9}
 ORDER = ("A", "B", "C", "D", "fk", "sm", "fj", "sl", "near", "sk")
-CLOSE_AT = (10, 18)
+PART_AT = 0
+WORK = {16: ("image", 0), 17: ("far", 0), 19: ("text", 1), 20: ("far", 1), 22: ("far", 2)}
 
 
 def coords(i):
@@ -87,7 +88,7 @@
 
 
 def kernel(scale_ref, bias_ref, ids_ref, img_ref, txt_ref, out_img, out_txt, close, fj, sk, sl, far, raw, coeff, ids,
-           far_ids, send_sem, recv_sem, part_sem, id_sem, own_sem):
+           far_ids, send_sem, recv_sem, id_sem, own_sem):
     me = lax.axis_index("dp")
     _, _, z, core = coords(me)
     s = side(core)
@@ -105,15 +106,15 @@
         "near": other_z(me, 1), "fix": wrap(me - 16 * s), "fj": other_z(me, -2), "fk": f_y(me, 1),
         "A": wrap(f_own + 86 * s), "B": wrap(f_own - 171 * s),
         "sk": s_y(me, 1), "sl": along_z(me, -2), "sm": along_z(me, -1),
-        "C": wrap(s_own3 - 86 * s), "D": wrap(s_own2 + 171 * s),
+        "C": wrap(s_own3 - 86 * s), "D": wrap(s_own2 + 171 * s), "part": wrap(me - s),
     }
     source = {
         "near": other_z(me, 1), "fix": wrap(me + 16 * s), "fj": other_z(me, -2), "fk": f_y(me, -1),
         "A": f_hold(wrap(me - 86 * s)), "B": f_hold(wrap(me - 171 * s)),
         "sk": s_y(me, -1), "sl": along_z(me, 2), "sm": along_z(me, 1),
-        "C": s_hold(wrap(me + 86 * s), 3), "D": s_hold(wrap(me + 171 * s), 2),
+        "C": s_hold(wrap(me + 86 * s), 3), "D": s_hold(wrap(me + 171 * s), 2), "part": wrap(me - s),
     }
-    partner = wrap(me - s)
+    partner = target["part"]
     id_to = [partner, wrap(me + s), wrap(me + 86 * s), wrap(me - 171 * s), wrap(me - 86 * s), wrap(me + 171 * s)]
     id_from = [partner, wrap(me + s), wrap(me - 86 * s), wrap(me - 171 * s), wrap(me + 86 * s), wrap(me + 171 * s)]
     only = {"fix": is_edge(z, core), "A": target["A"] != me, "C": target["C"] != me}
@@ -162,6 +163,8 @@
             return close.at[near_slot_there, rows]
         if leg == "fix":
             return close.at[2, rows]
+        if leg == "part":
+            return close.at[1, rows]
         if leg == "fk":
             return far_rows(a_there, i)
         if leg == "sm":
@@ -194,11 +197,6 @@
         else:
             getattr(remote(leg, i), what)()
 
-    def whole():
-        return pltpu.make_async_remote_copy(
-            src_ref=close.at[0], dst_ref=close.at[1], send_sem=part_sem.at[0], recv_sem=part_sem.at[1],
-            device_id=(partner,), device_id_type=MESH)
-
     def send_ids(j):
         return pltpu.make_async_remote_copy(
             src_ref=ids, dst_ref=far_ids.at[j], send_sem=id_sem.at[j], recv_sem=id_sem.at[6 + j],
@@ -209,7 +207,6 @@
         do("sk", i, "start")
     for j in range(6):
         send_ids(j).start()
-    whole().start()
 
     scale, bias = scale_ref[0], bias_ref[0]
     diagonal = lax.broadcasted_iota(jnp.int32, (ROWS, ROWS), 0) == lax.broadcasted_iota(jnp.int32, (ROWS, ROWS), 1)
@@ -218,10 +215,10 @@
     outs = (out_img, out_txt)
 
     def gain(a, key_rows, key_ids, first=False):
+        count = key_rows.shape[0]
         scores = lax.dot_general(close[0, pl.ds((1 - a) * ROWS, ROWS)], key_rows, (((1,), (1,)), ((), ())),
                                  preferred_element_type=jnp.float32)
         positive = (my_ids == key_ids).astype(jnp.float32)
-        count = key_rows.shape[0]
         coeff[:, pl.ds(0, count)] = (scale * (jax.nn.sigmoid(scale * scores + bias) - positive)).astype(jnp.bfloat16)
         term = jnp.dot(coeff[:, pl.ds(0, count)], key_rows, preferred_element_type=jnp.float32)
         if first:
@@ -231,11 +228,11 @@
 
     def close_step(a):
         if a == 0:
-            whole().wait_recv()
             for j in range(6):
                 send_ids(j).wait_recv()
         for i in range(a * CHUNKS // 2, (a + 1) * CHUNKS // 2):
             do("fix", i, "wait_recv")
+            do("part", i, "wait_recv")
         key_ids = jnp.concatenate([ids_ref[...], far_ids[0, pl.ds(0, 1)], far_ids[1, pl.ds(0, 1)]], axis=1)
         gain(a, close[pl.ds(0, 3), pl.ds(a * ROWS, ROWS)].reshape(3 * ROWS, D), key_ids, first=True)
 
@@ -245,25 +242,26 @@
         key_ids = jnp.concatenate([far_ids[j, pl.ds(0, 1), lanes] for j in range(2, 6)], axis=1)
         gain(a, far[part_of, pl.ds(0, 4 * HALF)], key_ids)
 
-    for t in range(CHUNKS + max(DELAY.values())):
+    last = max(DELAY.values())
+    for t in range(CHUNKS + last):
         for leg in ORDER:
             i = t - DELAY[leg]
             if 0 <= i < CHUNKS:
                 do(leg, i, "wait_recv")
                 for out in NEXT.get(leg, ()):
                     do(out, i, "start")
-        if t in CLOSE_AT:
-            close_step(CLOSE_AT.index(t))
-        i = t - max(DELAY.values())
-        if 0 <= i < CHUNKS - 1:
+        if 0 <= t - PART_AT < CHUNKS:
+            do("part", t - PART_AT, "start")
+        if t in WORK:
+            kind, which = WORK[t]
+            far_step(which) if kind == "far" else close_step(which)
+        if 0 <= t - last < CHUNKS - 1:
             for leg in LEGS:
-                do(leg, i, "wait_send")
-        if 0 <= i and (i + 1) % (HALF // SIZE) == 0:
-            far_step(i // (HALF // SIZE))
+                do(leg, t - last, "wait_send")
+    far_step(3)
 
     for leg in LEGS:
         do(leg, CHUNKS - 1, "wait_send")
-    whole().wait_send()
     for j in range(6):
         send_ids(j).wait_send()
 
@@ -312,7 +310,7 @@
             rows(4, 2 * ROWS, D), *[rows(2 * ROWS, D)] * 3, rows(4, 6 * HALF, D), rows(2, ROWS, D), rows(ROWS, 3 * ROWS),
             pltpu.VMEM((8, ROWS), jnp.int32), pltpu.VMEM((6, 8, ROWS), jnp.int32),
             pltpu.SemaphoreType.DMA((len(LEGS), CHUNKS)), pltpu.SemaphoreType.DMA((len(LEGS), CHUNKS)),
-            pltpu.SemaphoreType.DMA((2,)), pltpu.SemaphoreType.DMA((12,)), pltpu.SemaphoreType.DMA((2,)),
+            pltpu.SemaphoreType.DMA((12,)), pltpu.SemaphoreType.DMA((2,)),
         ],
         compiler_params=pltpu.CompilerParams(collective_id=0, has_side_effects=True, vmem_limit_bytes=VMEM_LIMIT),
         cost_estimate=pl.CostEstimate(flops=28 * ROWS * ROWS * D * 2, bytes_accessed=6 * ROWS * D * 4, transcendentals=14 * ROWS * ROWS),

time: 127 us -> 123 us (0.969)
  Pallas kernels: 125 us -> 121 us
    pallas_call x1, Pallas kernels: 122 us -> 118 us  [per_device(): pl.pallas_call(kernel, out_shape=(grad, grad), in_specs=[smem, smem, vmem...]
where the time goes in v3:
time: 123 us
  Pallas kernels  121 us (98%)
  between operations  1.93 us (2%)
    pallas_call x1, Pallas kernels, per_device(): pl.pallas_call(kernel, out_shape=(grad, grad), in_specs=[smem, smem, vmem...  118 us
    pallas_call x1, Pallas kernels, per_device(): pl.pallas_call(project, out_shape=(grad, grad), in_specs=[hbm] * 4, out_s...  3.15 us

profile of v3, /device:TPU:1, one launch (start us, length us, event | category | flops | bytes accessed | tf_op | source)
XLA Modules:
  0.0 122.8 jit_solution(7846989765356069675)
XLA Ops:
  1.9 117.7 %shard_map.68 = (f32[256,1152]{1,0:T(8,128)}, f32[256,1152]{1,0:T(8,128)}) custom-call(f32[1]{0:T(128)S(6)} %copy.7.scale_ref, f32[1]{0:T(128)S(6)} %copy.8.bias_ref, s32[1,256]{1,0:T(1,128)} %bitcast.1, bf16[256,1152]{1,0:T(8,128)(2,1)} %img.1, bf16[256,1152]{1,0:T(8,128)(2,1)} %txt.1), custom_call_target="tpu_custom_call" | custom-call | flops 4227858432 | bytes 7077888 | tf_op jit(solution)/shard_map/pallas_call | solution.py:304
  119.7 3.2 %shard_map.69 = (f32[256,1152]{1,0:T(8,128)}, f32[256,1152]{1,0:T(8,128)}) custom-call(f32[256,1152]{1,0:T(8,128)} %get-tuple-element.4.grad_img, f32[256,1152]{1,0:T(8,128)} %get-tuple-element.5.grad_txt, bf16[256,1152]{1,0:T(8,128)(2,1)} %img.1, bf16[256,1152]{1,0:T(8,128)(2,1)} %txt.1), custom_call_target="tpu_custom_call" | custom-call | flops 4718592 | bytes 5898240 | tf_op jit(solution)/shard_map/pallas_call | solution.py:318

commit v4 on v3

--- a/solution.py
+++ b/solution.py
@@ -13,12 +13,13 @@
 SIZE = 2 * ROWS // CHUNKS
 HALF = 128
 NORM_ROWS = 64
-PROJECT_ROWS = 64
+PROJECT_ROWS = 128
 VMEM_LIMIT = 56 * 2**20
 LEGS = ("near", "fix", "fj", "fk", "A", "B", "sk", "sl", "sm", "C", "D", "part")
 NEXT = {"near": ("fj", "fix"), "sk": ("sl",), "fj": ("fk",), "sl": ("sm", "D"), "fk": ("A", "B"), "sm": ("C",)}
 DELAY = {"near": 0, "sk": 0, "fj": 3, "sl": 3, "fk": 6, "sm": 6, "A": 9, "B": 9, "C": 9, "D": 9}
 ORDER = ("A", "B", "C", "D", "fk", "sm", "fj", "sl", "near", "sk")
+FAR_IDS = 7
 PART_AT = 0
 WORK = {16: ("image", 0), 17: ("far", 0), 19: ("text", 1), 20: ("far", 1), 22: ("far", 2)}
 
@@ -88,7 +89,7 @@
 
 
 def kernel(scale_ref, bias_ref, ids_ref, img_ref, txt_ref, out_img, out_txt, close, fj, sk, sl, far, raw, coeff, ids,
-           far_ids, send_sem, recv_sem, id_sem, own_sem):
+           send_sem, recv_sem, id_sem, own_sem):
     me = lax.axis_index("dp")
     _, _, z, core = coords(me)
     s = side(core)
@@ -114,9 +115,6 @@
         "sk": s_y(me, -1), "sl": along_z(me, 2), "sm": along_z(me, 1),
         "C": s_hold(wrap(me + 86 * s), 3), "D": s_hold(wrap(me + 171 * s), 2), "part": wrap(me - s),
     }
-    partner = target["part"]
-    id_to = [partner, wrap(me + s), wrap(me + 86 * s), wrap(me - 171 * s), wrap(me - 86 * s), wrap(me + 171 * s)]
-    id_from = [partner, wrap(me + s), wrap(me - 86 * s), wrap(me - 171 * s), wrap(me + 86 * s), wrap(me + 171 * s)]
     only = {"fix": is_edge(z, core), "A": target["A"] != me, "C": target["C"] != me}
     passes = {leg: jnp.where(where, 1, 0) for leg, where in only.items()}
 
@@ -126,8 +124,6 @@
     always = [leg for leg in LEGS if leg not in only]
     for leg in always:
         signal(source[leg])
-    for device in id_from:
-        signal(device)
     for leg, where in only.items():
         pl.when(where)(lambda leg=leg: signal(source[leg]))
 
@@ -141,9 +137,9 @@
             close[0, pl.ds(a * ROWS + first, NORM_ROWS)] = (values * (1.0 / norms)).astype(jnp.bfloat16)
             return carry
         lax.fori_loop(0, ROWS // NORM_ROWS, body, 0)
-    ids[...] = jnp.broadcast_to(ids_ref[...], (8, ROWS))
-
-    pl.semaphore_wait(barrier, len(always) + len(id_from) + sum(passes.values()))
+    ids[0] = jnp.broadcast_to(ids_ref[...], (8, ROWS))
+
+    pl.semaphore_wait(barrier, len(always) + sum(passes.values()))
 
     _, _, next_z, next_core = coords(target["near"])
     near_slot = 2 + passes["fix"]
@@ -182,6 +178,16 @@
             return far_rows(c_here, i)
         return to(leg, i)
 
+    def id_slot_to(leg):
+        far_slot = {"fk": a_there, "sm": c_there, "A": 0, "B": 1, "C": 2, "D": 3}
+        if leg in far_slot:
+            return FAR_IDS + far_slot[leg]
+        return {"near": near_slot_there, "fix": 2, "part": 1, "fj": 4, "sk": 5, "sl": 6}[leg]
+
+    def id_slot_at(leg):
+        here = {"near": near_slot, "fk": FAR_IDS + a_here, "sm": FAR_IDS + c_here}
+        return here[leg] if leg in here else id_slot_to(leg)
+
     came_by = {out: leg for leg, outs in NEXT.items() for out in outs}
 
     def remote(leg, i):
@@ -191,22 +197,25 @@
             dst_ref=to(leg, i), send_sem=send_sem.at[j, i], recv_sem=recv_sem.at[j, i],
             device_id=(target[leg],), device_id_type=MESH)
 
+    def remote_ids(leg):
+        j = LEGS.index(leg)
+        return pltpu.make_async_remote_copy(
+            src_ref=ids.at[id_slot_at(came_by[leg]) if leg in came_by else 0], dst_ref=ids.at[id_slot_to(leg)],
+            send_sem=id_sem.at[0, j], recv_sem=id_sem.at[1, j], device_id=(target[leg],), device_id_type=MESH)
+
     def do(leg, i, what):
+        def act():
+            if i == 0:
+                getattr(remote_ids(leg), what)()
+            getattr(remote(leg, i), what)()
         if leg in only:
-            pl.when(only[leg])(lambda: getattr(remote(leg, i), what)())
+            pl.when(only[leg])(act)
         else:
-            getattr(remote(leg, i), what)()
-
-    def send_ids(j):
-        return pltpu.make_async_remote_copy(
-            src_ref=ids, dst_ref=far_ids.at[j], send_sem=id_sem.at[j], recv_sem=id_sem.at[6 + j],
-            device_id=(id_to[j],), device_id_type=MESH)
+            act()
 
     for i in range(CHUNKS):
         do("near", i, "start")
         do("sk", i, "start")
-    for j in range(6):
-        send_ids(j).start()
 
     scale, bias = scale_ref[0], bias_ref[0]
     diagonal = lax.broadcasted_iota(jnp.int32, (ROWS, ROWS), 0) == lax.broadcasted_iota(jnp.int32, (ROWS, ROWS), 1)
@@ -227,19 +236,16 @@
             outs[a][...] += term
 
     def close_step(a):
-        if a == 0:
-            for j in range(6):
-                send_ids(j).wait_recv()
         for i in range(a * CHUNKS // 2, (a + 1) * CHUNKS // 2):
             do("fix", i, "wait_recv")
             do("part", i, "wait_recv")
-        key_ids = jnp.concatenate([ids_ref[...], far_ids[0, pl.ds(0, 1)], far_ids[1, pl.ds(0, 1)]], axis=1)
+        key_ids = jnp.concatenate([ids[j, pl.ds(0, 1)] for j in range(3)], axis=1)
         gain(a, close[pl.ds(0, 3), pl.ds(a * ROWS, ROWS)].reshape(3 * ROWS, D), key_ids, first=True)
 
     def far_step(part_of):
         a, half = part_of // 2, part_of % 2
         lanes = pl.ds(half * HALF, HALF)
-        key_ids = jnp.concatenate([far_ids[j, pl.ds(0, 1), lanes] for j in range(2, 6)], axis=1)
+        key_ids = jnp.concatenate([ids[FAR_IDS + j, pl.ds(0, 1), lanes] for j in range(4)], axis=1)
         gain(a, far[part_of, pl.ds(0, 4 * HALF)], key_ids)
 
     last = max(DELAY.values())
@@ -262,8 +268,6 @@
 
     for leg in LEGS:
         do(leg, CHUNKS - 1, "wait_send")
-    for j in range(6):
-        send_ids(j).wait_send()
 
 
 def project(grad_img, grad_txt, img, txt, out_img, out_txt, grads, raw, result, sem):
@@ -308,9 +312,9 @@
         out_specs=(vmem, vmem),
         scratch_shapes=[
             rows(4, 2 * ROWS, D), *[rows(2 * ROWS, D)] * 3, rows(4, 6 * HALF, D), rows(2, ROWS, D), rows(ROWS, 3 * ROWS),
-            pltpu.VMEM((8, ROWS), jnp.int32), pltpu.VMEM((6, 8, ROWS), jnp.int32),
+            pltpu.VMEM((FAR_IDS + 6, 8, ROWS), jnp.int32),
             pltpu.SemaphoreType.DMA((len(LEGS), CHUNKS)), pltpu.SemaphoreType.DMA((len(LEGS), CHUNKS)),
-            pltpu.SemaphoreType.DMA((12,)), pltpu.SemaphoreType.DMA((2,)),
+            pltpu.SemaphoreType.DMA((2, len(LEGS))), pltpu.SemaphoreType.DMA((2,)),
         ],
         compiler_params=pltpu.CompilerParams(collective_id=0, has_side_effects=True, vmem_limit_bytes=VMEM_LIMIT),
         cost_estimate=pl.CostEstimate(flops=28 * ROWS * ROWS * D * 2, bytes_accessed=6 * ROWS * D * 4, transcendentals=14 * ROWS * ROWS),

time: 123 us -> 123 us (level)
  no operation moved by 1% of the time
where the time goes in v4:
time: 123 us
  Pallas kernels  121 us (98%)
  between operations  1.93 us (2%)
    pallas_call x1, Pallas kernels, per_device(): pl.pallas_call(kernel, out_shape=(grad, grad), in_specs=[smem, smem, vmem...  118 us
    pallas_call x1, Pallas kernels, per_device(): pl.pallas_call(project, out_shape=(grad, grad), in_specs=[hbm] * 4, out_s...  3.07 us

profile of v4, /device:TPU:1, one launch (start us, length us, event | category | flops | bytes accessed | tf_op | source)
XLA Modules:
  0.0 122.8 jit_solution(17664721125686308022)
XLA Ops:
  1.9 117.8 %shard_map.68 = (f32[256,1152]{1,0:T(8,128)}, f32[256,1152]{1,0:T(8,128)}) custom-call(f32[1]{0:T(128)S(6)} %copy.7.scale_ref, f32[1]{0:T(128)S(6)} %copy.8.bias_ref, s32[1,256]{1,0:T(1,128)} %bitcast.1, bf16[256,1152]{1,0:T(8,128)(2,1)} %img.1, bf16[256,1152]{1,0:T(8,128)(2,1)} %txt.1), custom_call_target="tpu_custom_call" | custom-call | flops 4227858432 | bytes 7077888 | tf_op jit(solution)/shard_map/pallas_call | solution.py:308
  119.7 3.1 %shard_map.69 = (f32[256,1152]{1,0:T(8,128)}, f32[256,1152]{1,0:T(8,128)}) custom-call(f32[256,1152]{1,0:T(8,128)} %get-tuple-element.4.grad_img, f32[256,1152]{1,0:T(8,128)} %get-tuple-element.5.grad_txt, bf16[256,1152]{1,0:T(8,128)(2,1)} %img.1, bf16[256,1152]{1,0:T(8,128)(2,1)} %txt.1), custom_call_target="tpu_custom_call" | custom-call | flops 4718592 | bytes 5898240 | tf_op jit(solution)/shard_map/pallas_call | solution.py:322
